TPU v7x, 32 devices: a whole 2x2x4 slice. The times are simulated.
32 devices in a mesh: grp: 2 (over x), ex: 16 (over z, y, core).
Axes of the slice: x: 2, y: 2, z: 4, core: 2. Of those that a mesh axis runs over, the one named last changes fastest.
Arguments:
- queries: bfloat16 [2, 32, 4, 1536], P(None, ('grp', 'ex')), parts along dimension 1, may hold values from -8 to 8
- keys: bfloat16 [2, 32, 4, 2, 256, 128], P(None, ('grp', 'ex')), parts along dimension 1, may hold values from -8 to 8
- values: bfloat16 [2, 32, 4, 2, 256, 128], P(None, ('grp', 'ex')), parts along dimension 1, may hold values from -6 to 6
- lengths: int32 [2, 32], P(None, ('grp', 'ex')), parts along dimension 1, may hold values from 1 to 256, 2048 in all within a row
- routes: int32 [2, 32, 4], P(None, ('grp', 'ex')), parts along dimension 1, may hold values from 0 to 7, all different within a row
- residual: bfloat16 [2, 32, 6144], P(None, ('grp', 'ex')), parts along dimension 1, may hold values from -6 to 6
- gain: bfloat16 [6144], replicated, may hold values from 0.099609375 to 1.8984375
- w_router: bfloat16 [6144, 8], replicated, may hold values from -0.3125 to 0.3125
- w_in: bfloat16 [16, 6144, 2688], P('ex'), may hold values from -0.078125 to 0.078125
- w_out: bfloat16 [16, 2688, 6144], P('ex'), may hold values from -0.078125 to 0.078125
Outputs:
- layer_out: bfloat16 [2, 32, 6144], P(None, ('grp', 'ex')), parts along dimension 1
There are 2 independent parts, one for each index of `grp`. A program takes and returns all parts, laid end to end along the dimension named above; an argument that names none is the same for every part. Nothing has to cross between parts.
Inputs may be any that keep to these rules, and one draw needn't show every extreme that they name: `routes`: each row names 4 different experts. The lengths of the rows of each micro-batch sum to 2048, and in each micro-batch some row uses all 256 positions.
All inputs are finite; a program needn't handle non-finite values. No bound on the sum of `lengths` on one device may be relied on, other than what follows from the above.
Results may differ from a plain program's by a relative error of at most 0.0045.
Values may be sent and summed in bfloat16 or wider, within the bound.
A program may use at most 192 MiB of HBM per device.

v0:
```python
import math

import jax
import jax.numpy as jnp
from jax import lax
from jax.sharding import PartitionSpec as P

HD = 128
EXPERTS = 8


def swapped(value, axis, stride):
    mask = 2**stride
    pairs = [(source, source ^ mask) for source in range(lax.axis_size(axis))]
    return lax.ppermute(value, axis, pairs)


def attend(query_rows, key_rows, value_rows, group_len):
    groups, heads_flat = query_rows.shape
    kv_heads = key_rows.shape[1]
    span = key_rows.shape[2]
    per_kv = heads_flat // (kv_heads * HD)
    query_heads = query_rows.reshape(groups, kv_heads, per_kv, HD)
    scores = jnp.einsum(
        "gkqd,gkld->gkql", query_heads, key_rows, preferred_element_type=jnp.float32
    ) / math.sqrt(HD)
    position = lax.broadcasted_iota(jnp.int32, (groups, 1, 1, span), 3)
    valid = position < group_len[:, None, None, None]
    masked = jnp.where(valid, scores, -1e30)
    top = jnp.max(masked, axis=-1, keepdims=True)
    expo = jnp.where(valid, jnp.exp(masked - top), 0.0)
    probs = (expo / jnp.sum(expo, axis=-1, keepdims=True)).astype(jnp.bfloat16)
    context = jnp.einsum("gkql,gkld->gkqd", probs, value_rows, preferred_element_type=jnp.float32)
    return context.astype(jnp.bfloat16).reshape(groups, heads_flat)


def expert_rows(rows, weight_in, weight_out):
    leading = rows.shape[:-1]
    flat = rows.reshape(-1, rows.shape[-1])
    hidden = jax.nn.silu(jnp.dot(flat, weight_in, preferred_element_type=jnp.float32)).astype(
        jnp.bfloat16
    )
    return jnp.dot(hidden, weight_out, preferred_element_type=jnp.float32).reshape(
        leading + (weight_out.shape[-1],)
    )


def on_device(queries, keys, values, lengths, routes, residual, gain, w_router, w_in, w_out):
    width = lax.axis_size("ex")
    index = lax.axis_index("ex")
    split = width // EXPERTS
    micro_count = queries.shape[0]
    row_dev = residual.shape[1]
    model = residual.shape[2]
    quarter = index & 3
    weight_in = w_in[0]
    weight_out = w_out[0]
    group_len = lengths
    for bit in range(2):
        upper = index >> bit & 1 == 1
        other = swapped(group_len, "ex", bit)
        group_len = jnp.where(
            upper, jnp.concatenate([other, group_len], 1), jnp.concatenate([group_len, other], 1)
        )
    outputs = []
    for micro in range(micro_count):
        context = attend(queries[micro, 0], keys[micro, 0], values[micro, 0], group_len[micro])
        whole = context
        for bit in range(2):
            upper = index >> bit & 1 == 1
            other = swapped(whole, "ex", bit)
            whole = jnp.where(
                upper, jnp.concatenate([other, whole], 1), jnp.concatenate([whole, other], 1)
            )
        own_context = lax.dynamic_slice_in_dim(whole, quarter * row_dev, row_dev, 0)
        state = residual[micro].astype(jnp.float32) + own_context.astype(jnp.float32)
        scale = lax.rsqrt(jnp.mean(state * state, axis=-1, keepdims=True) + 1e-05)
        normed = (state * scale * gain.astype(jnp.float32)).astype(jnp.bfloat16)
        logits = jnp.dot(normed, w_router, preferred_element_type=jnp.float32)
        chosen = routes[micro][:, :, None] == lax.broadcasted_iota(jnp.int32, (1, 1, EXPERTS), 2)
        picked = jnp.sum(jnp.where(chosen, logits[:, None, :], 0.0), axis=-1)
        gates = jax.nn.sigmoid(picked)
        shares = gates / jnp.sum(gates, axis=-1, keepdims=True)
        mix = jnp.sum(jnp.where(chosen, shares[:, :, None], 0.0), axis=1)
        used = jnp.any(chosen, axis=1).T
        blank = jnp.zeros((), jnp.bfloat16)
        routed = jnp.where(used[:, None, :, None], normed[None, None, :, :], blank)
        outgoing = jnp.broadcast_to(routed, (EXPERTS, split, row_dev, model)).reshape(
            width, row_dev, model
        )
        partials = expert_rows(
            lax.all_to_all(outgoing, "ex", split_axis=0, concat_axis=0, tiled=True),
            weight_in,
            weight_out,
        )
        returned = lax.all_to_all(
            partials.astype(jnp.bfloat16), "ex", split_axis=0, concat_axis=0, tiled=True
        ).astype(partials.dtype)
        expert_out = jnp.sum(returned.reshape(EXPERTS, split, row_dev, model), axis=1)
        mixed = state + jnp.sum(mix.T[:, :, None] * expert_out, axis=0)
        outputs.append(mixed.astype(jnp.bfloat16))
    return jnp.stack(outputs, axis=0)


def solution(mesh):
    return jax.shard_map(
        on_device,
        mesh=mesh,
        in_specs=(
            P(None, ("grp", "ex"), None, None),
            P(None, ("grp", "ex"), None, None, None, None),
            P(None, ("grp", "ex"), None, None, None, None),
            P(None, ("grp", "ex")),
            P(None, ("grp", "ex"), None),
            P(None, ("grp", "ex"), None),
            P(),
            P(),
            P("ex", None, None),
            P("ex", None, None),
        ),
        out_specs=P(None, ("grp", "ex"), None),
        check_vma=False,
    )
```

profile of v0, /device:TPU:0, one launch (start us, length us, event | category | flops | bytes accessed | tf_op | source)
XLA Modules:
  0.0 118.4 jit_solution(1086791908640016725)
XLA Ops:
  2.7 2.6 %collective-permute-start.1 = (s32[2,2]{0,1:T(2,128)S(1)}, s32[2,2]{0,1:T(2,128)S(1)}, u32[]{:S(2)}, u32[]{:S(2)}) collective-permute-start(s32[2,2]{0,1:T(2,128)S(1)} %add_select_fusion.1), channel_id=1, source_target_pairs={{0,2},{1,3},{2,0},{3,1},{4,6},{5,7},{6,4},{7,5},{8,10},{9,11},{10,... | collective-permute-start | bytes 56 | tf_op jit(solution)/shard_map/ppermute | solution.py:15
  5.2 1.5 %collective-permute-done.1 = s32[2,2]{0,1:T(2,128)S(1)} collective-permute-done((s32[2,2]{0,1:T(2,128)S(1)}, s32[2,2]{0,1:T(2,128)S(1)}, u32[]{:S(2)}, u32[]{:S(2)}) %collective-permute-start.1) | collective-permute-done | bytes 48 | tf_op jit(solution)/shard_map/ppermute | solution.py:15
  7.1 1.3 %fusion.29 = f32[4,2,6,256]{3,2,1,0:T(8,128)S(1)} fusion(bf16[4,2,6,128]{3,2,1,0:T(8,128)(2,1)S(1)} %reshape_squeeze.7, bf16[2,1,4,2,256,128]{5,4,3,2,1,0:T(8,128)(2,1)} %param.11, pred[4,256]{1,0:T(4,128)(4,1)S(1)} %get-tuple-element.19), kind=kOutput, calls=%fused_computation.23 | convolution fusion | flops 3170304 | bytes 586752 | tf_op jit(solution)/shard_map/gkqd,gkld->gkql/dot_general | solution.py:24
  8.5 1.3 %convolution_convert_fusion = bf16[4,2,6,128]{3,2,1,0:T(8,128)(2,1)S(1)} fusion(bf16[2,1,4,2,256,128]{5,4,3,2,1,0:T(8,128)(2,1)} %param.12, f32[4,2,6]{2,1,0:T(2,128)S(1)} %fusion.84, f32[4,2,6,256]{3,2,1,0:T(8,128)S(1)} %fusion.29, pred[4,256]{1,0:T(4,128)(4,1)S(1)} %get-tuple-element.19), kind=kOutput, calls=%fused_computation.24 | convolution fusion | flops 3201327 | bytes 672768 | tf_op jit(solution)/shard_map/gkql,gkld->gkqd/dot_general | solution.py:33
  9.9 1.3 %fusion.28 = f32[4,2,6,256]{3,2,1,0:T(8,128)S(1)} fusion(bf16[4,2,6,128]{3,2,1,0:T(8,128)(2,1)S(1)} %reshape_squeeze.6, bf16[2,1,4,2,256,128]{5,4,3,2,1,0:T(8,128)(2,1)} %param.11, pred[4,256]{1,0:T(4,128)(4,1)S(1)} %get-tuple-element.20), kind=kOutput, calls=%fused_computation.22 | convolution fusion | flops 3170304 | bytes 586752 | tf_op jit(solution)/shard_map/gkqd,gkld->gkql/dot_general | solution.py:24
  11.4 1.3 %convolution_convert_fusion.1 = bf16[4,2,6,128]{3,2,1,0:T(8,128)(2,1)S(1)} fusion(bf16[2,1,4,2,256,128]{5,4,3,2,1,0:T(8,128)(2,1)} %param.12, f32[4,2,6]{2,1,0:T(2,128)S(1)} %fusion.83, f32[4,2,6,256]{3,2,1,0:T(8,128)S(1)} %fusion.28, pred[4,256]{1,0:T(4,128)(4,1)S(1)} %get-tuple-element.20), kind=kOutput, calls=%fused_computation.25 | convolution fusion | flops 3201327 | bytes 672768 | tf_op jit(solution)/shard_map/gkql,gkld->gkqd/dot_general | solution.py:33
  13.3 2.1 %collective-permute-start.5 = (bf16[4,3072]{1,0:T(4,128)(2,1)S(1)}, bf16[4,3072]{1,0:T(4,128)(2,1)S(1)}, u32[]{:S(2)}, u32[]{:S(2)}) collective-permute-start(bf16[4,3072]{1,0:T(4,128)(2,1)S(1)} %maximum_select_fusion.1), channel_id=1, source_target_pairs={{0,2},{1,3},{2,0},{3,1},{4,6},{5,7},{6,4},{7,5},{8,10},{9,11},{10,... | collective-permute-start | bytes 73736 | tf_op jit(solution)/shard_map/ppermute | solution.py:15
  15.4 0.8 collective-permute-start.3
  17.2 2.1 %collective-permute-done.3 = bf16[4,3072]{1,0:T(4,128)(2,1)S(1)} collective-permute-done((bf16[4,3072]{1,0:T(4,128)(2,1)S(1)}, bf16[4,3072]{1,0:T(4,128)(2,1)S(1)}, u32[]{:S(2)}, u32[]{:S(2)}) %collective-permute-start.3) | collective-permute-done | bytes 24608 | tf_op jit(solution)/shard_map/ppermute | solution.py:15
  19.3 1.7 %multiply_reduce_fusion.1 = (f32[]{:T(128)}, f32[1,6144]{1,0:T(1,128)S(1)}, f32[]{:T(128)}, f32[1,6144]{1,0:T(1,128)S(1)}) fusion(s32[]{:T(128)S(6)} %select_n.130, bf16[4,3072]{1,0:T(4,128)(2,1)S(1)} %collective-permute-done.3, bf16[4,3072]{1,0:T(4,128)(2,1)S(1)} %maximum_select_fusion, pred[]{:T(512)S(6)} %eq.72, bf16[2,1,6144]{2,0,1:T(2,128)(2,1)} %param.15, ...), kind=kLoop, calls=%fused_computation.88 | loop fusion | flops 172030 | bytes 172045 | tf_op jit(solution)/shard_map/reduce_sum | solution.py:77
  23.8 1.8 %reduce.30 = bf16[16,6144]{1,0:T(8,128)(2,1)S(1)} reduce(bf16[16,1,6144]{2,1,0:T(2,128)(2,1)S(1)} %broadcast_in_dim.149, bf16[]{:T(256)} %broadcast.422), dimensions={1}, to_apply=%broadcast_in_dim.149.reduce_sub_computation | reduce | bytes 393218 | tf_op jit(solution)/shard_map/broadcast_in_dim | solution.py:88
  26.4 5.2 %all-to-all-start = ((bf16[16,2,3072]{2,1,0:T(2,128)(2,1)}), bf16[16,2,3072]{2,1,0:T(2,128)(2,1)S(1)}, u32[]{:S(2)}, u32[]{:S(2)}) async-start(bf16[16,2,3072]{2,1,0:T(2,128)(2,1)} %reshape.679), calls=%async_computation | async-start | bytes 393216 | tf_op jit(solution)/shard_map/all_to_all | solution.py:92
  34.4 1.8 %reduce.28 = bf16[16,6144]{1,0:T(8,128)(2,1)S(1)} reduce(bf16[16,1,6144]{2,1,0:T(2,128)(2,1)S(1)} %broadcast_in_dim.150, bf16[]{:T(256)} %broadcast.422), dimensions={1}, to_apply=%broadcast_in_dim.150.reduce_sub_computation | reduce | bytes 393218 | tf_op jit(solution)/shard_map/broadcast_in_dim | solution.py:88
  36.1 0.8 reshape.675
  37.7 2.9 %all-to-all-done = bf16[16,2,3072]{2,1,0:T(2,128)(2,1)S(1)} async-done(((bf16[16,2,3072]{2,1,0:T(2,128)(2,1)}), bf16[16,2,3072]{2,1,0:T(2,128)(2,1)S(1)}, u32[]{:S(2)}, u32[]{:S(2)}) %all-to-all-start) | async-done | bytes 196640 | tf_op jit(solution)/shard_map/all_to_all | solution.py:92
  40.5 3.5 %all-to-all-start.2 = ((bf16[16,2,3072]{2,1,0:T(2,128)(2,1)}), bf16[16,2,3072]{2,1,0:T(2,128)(2,1)S(1)}, u32[]{:S(2)}, u32[]{:S(2)}) async-start(bf16[16,2,3072]{2,1,0:T(2,128)(2,1)} %reshape.675), calls=%async_computation.2 | async-start | bytes 393216 | tf_op jit(solution)/shard_map/all_to_all | solution.py:92
  44.2 23.6 %fusion.19 = bf16[16,1,6144]{2,0,1:T(8,128)(2,1)S(1)} fusion(bf16[1,2688,6144]{2,1,0:T(8,128)(2,1)} %param.19, bf16[1,6144,2688]{2,1,0:T(8,128)(2,1)} %param.18, bf16[16,1,6144]{2,1,0:T(2,128)(2,1)S(1)} %reshape.680), kind=kOutput, calls=%fused_computation.13 | convolution fusion | flops 1057277952 | bytes 66453504 | tf_op jit(solution)/shard_map/dot_general | solution.py:43
  69.4 6.0 %all-to-all-start.1 = ((bf16[16,2,3072]{2,1,0:T(2,128)(2,1)}), bf16[16,2,3072]{2,1,0:T(2,128)(2,1)S(1)}, u32[]{:S(2)}, u32[]{:S(2)}) async-start(bf16[16,2,3072]{2,1,0:T(2,128)(2,1)} %reshape.681), calls=%async_computation.1 | async-start | bytes 393216 | tf_op jit(solution)/shard_map/all_to_all | solution.py:96
  75.5 23.6 %fusion.16 = bf16[16,1,6144]{2,0,1:T(8,128)(2,1)S(1)} fusion(bf16[1,2688,6144]{2,1,0:T(8,128)(2,1)} %param.19, bf16[1,6144,2688]{2,1,0:T(8,128)(2,1)} %param.18, bf16[16,1,6144]{2,1,0:T(2,128)(2,1)S(1)} %reshape.676), kind=kOutput, calls=%fused_computation.12 | convolution fusion | flops 1057277952 | bytes 66453504 | tf_op jit(solution)/shard_map/dot_general | solution.py:43
  99.8 0.8 reshape.677
  100.7 6.0 %all-to-all-start.3 = ((bf16[16,2,3072]{2,1,0:T(2,128)(2,1)}), bf16[16,2,3072]{2,1,0:T(2,128)(2,1)S(1)}, u32[]{:S(2)}, u32[]{:S(2)}) async-start(bf16[16,2,3072]{2,1,0:T(2,128)(2,1)} %reshape.677), calls=%async_computation.3 | async-start | bytes 393216 | tf_op jit(solution)/shard_map/all_to_all | solution.py:96
  106.8 1.1 convert_reduce_fusion.1
  108.8 6.9 %all-to-all-done.3 = bf16[16,2,3072]{2,1,0:T(2,128)(2,1)S(1)} async-done(((bf16[16,2,3072]{2,1,0:T(2,128)(2,1)}), bf16[16,2,3072]{2,1,0:T(2,128)(2,1)S(1)}, u32[]{:S(2)}, u32[]{:S(2)}) %all-to-all-start.3) | async-done | bytes 196640 | tf_op jit(solution)/shard_map/all_to_all | solution.py:96
  115.8 1.1 convert_reduce_fusion
  (64 shorter events, 15.9 us)
Async XLA Ops:
  0.0 22.4 %copy-start = (bf16[6144,8]{0,1:T(8,128)(2,1)S(1)}, bf16[6144,8]{0,1:T(8,128)(2,1)}, u32[]{:S(2)}) copy-start(bf16[6144,8]{0,1:T(8,128)(2,1)} %param.17) | copy-start | bytes 294916
  0.0 1.9 %collective-permute-start = (s32[2,1]{0,1:T(1,128)}, s32[2,1]{0,1:T(1,128)S(1)}, u32[]{:S(2)}, u32[]{:S(2)}) collective-permute-start(s32[2,1]{0,1:T(1,128)} %param.13), channel_id=1, source_target_pairs={{0,1},{1,0},{2,3},{3,2},{4,5},{5,4},{6,7},{7,6},{8,9},{9,8},{10,11... | collective-permute-start | bytes 32 | tf_op jit(solution)/shard_map/ppermute | solution.py:15
  2.7 4.1 %collective-permute-start.1 = (s32[2,2]{0,1:T(2,128)S(1)}, s32[2,2]{0,1:T(2,128)S(1)}, u32[]{:S(2)}, u32[]{:S(2)}) collective-permute-start(s32[2,2]{0,1:T(2,128)S(1)} %add_select_fusion.1), channel_id=1, source_target_pairs={{0,2},{1,3},{2,0},{3,1},{4,6},{5,7},{6,4},{7,5},{8,10},{9,11},{10,... | collective-permute-start | bytes 56 | tf_op jit(solution)/shard_map/ppermute | solution.py:15
  9.9 3.4 %collective-permute-start.4 = (bf16[4,1536]{1,0:T(4,128)(2,1)S(1)}, bf16[4,1536]{1,0:T(4,128)(2,1)S(1)}, u32[]{:S(2)}, u32[]{:S(2)}) collective-permute-start(bf16[4,1536]{1,0:T(4,128)(2,1)S(1)} %reshape.649), channel_id=1, source_target_pairs={{0,1},{1,0},{2,3},{3,2},{4,5},{5,4},{6,7},{7,6},{8,9},{9,8},{10,11... | collective-permute-start | bytes 36872 | tf_op jit(solution)/shard_map/ppermute | solution.py:15
  12.7 2.7 %collective-permute-start.2 = (bf16[4,1536]{1,0:T(4,128)(2,1)S(1)}, bf16[4,1536]{1,0:T(4,128)(2,1)S(1)}, u32[]{:S(2)}, u32[]{:S(2)}) collective-permute-start(bf16[4,1536]{1,0:T(4,128)(2,1)S(1)} %reshape.644), channel_id=1, source_target_pairs={{0,1},{1,0},{2,3},{3,2},{4,5},{5,4},{6,7},{7,6},{8,9},{9,8},{10,11... | collective-permute-start | bytes 36872 | tf_op jit(solution)/shard_map/ppermute | solution.py:15
  13.3 3.9 %collective-permute-start.5 = (bf16[4,3072]{1,0:T(4,128)(2,1)S(1)}, bf16[4,3072]{1,0:T(4,128)(2,1)S(1)}, u32[]{:S(2)}, u32[]{:S(2)}) collective-permute-start(bf16[4,3072]{1,0:T(4,128)(2,1)S(1)} %maximum_select_fusion.1), channel_id=1, source_target_pairs={{0,2},{1,3},{2,0},{3,1},{4,6},{5,7},{6,4},{7,5},{8,10},{9,11},{10,... | collective-permute-start | bytes 73736 | tf_op jit(solution)/shard_map/ppermute | solution.py:15
  15.4 3.9 %collective-permute-start.3 = (bf16[4,3072]{1,0:T(4,128)(2,1)S(1)}, bf16[4,3072]{1,0:T(4,128)(2,1)S(1)}, u32[]{:S(2)}, u32[]{:S(2)}) collective-permute-start(bf16[4,3072]{1,0:T(4,128)(2,1)S(1)} %maximum_select_fusion), channel_id=1, source_target_pairs={{0,2},{1,3},{2,0},{3,1},{4,6},{5,7},{6,4},{7,5},{8,10},{9,11},{10,... | collective-permute-start | bytes 73736 | tf_op jit(solution)/shard_map/ppermute | solution.py:15
  26.4 14.2 %all-to-all-start = ((bf16[16,2,3072]{2,1,0:T(2,128)(2,1)}), bf16[16,2,3072]{2,1,0:T(2,128)(2,1)S(1)}, u32[]{:S(2)}, u32[]{:S(2)}) async-start(bf16[16,2,3072]{2,1,0:T(2,128)(2,1)} %reshape.679), calls=%async_computation | async-start | bytes 393216 | tf_op jit(solution)/shard_map/all_to_all | solution.py:92
  40.5 28.8 %all-to-all-start.2 = ((bf16[16,2,3072]{2,1,0:T(2,128)(2,1)}), bf16[16,2,3072]{2,1,0:T(2,128)(2,1)S(1)}, u32[]{:S(2)}, u32[]{:S(2)}) async-start(bf16[16,2,3072]{2,1,0:T(2,128)(2,1)} %reshape.675), calls=%async_computation.2 | async-start | bytes 393216 | tf_op jit(solution)/shard_map/all_to_all | solution.py:92
  69.4 31.3 %all-to-all-start.1 = ((bf16[16,2,3072]{2,1,0:T(2,128)(2,1)}), bf16[16,2,3072]{2,1,0:T(2,128)(2,1)S(1)}, u32[]{:S(2)}, u32[]{:S(2)}) async-start(bf16[16,2,3072]{2,1,0:T(2,128)(2,1)} %reshape.681), calls=%async_computation.1 | async-start | bytes 393216 | tf_op jit(solution)/shard_map/all_to_all | solution.py:96
  75.4 43.1 %copy-start.1 = (bf16[6144,8]{0,1:T(8,128)(2,1)S(1)}, bf16[6144,8]{0,1:T(8,128)(2,1)}, u32[]{:S(2)}) copy-start(bf16[6144,8]{0,1:T(8,128)(2,1)} %param.17) | copy-start | bytes 294916
  100.7 15.0 %all-to-all-start.3 = ((bf16[16,2,3072]{2,1,0:T(2,128)(2,1)}), bf16[16,2,3072]{2,1,0:T(2,128)(2,1)S(1)}, u32[]{:S(2)}, u32[]{:S(2)}) async-start(bf16[16,2,3072]{2,1,0:T(2,128)(2,1)} %reshape.677), calls=%async_computation.3 | async-start | bytes 393216 | tf_op jit(solution)/shard_map/all_to_all | solution.py:96
where the time goes:
time: 119 us; the launch traced here: 118 us
  matrix products  52.6 us (44%)
  starting transfers between devices  27.2 us (23%)
  other arithmetic  16.3 us (14%)
  waiting for transfers between devices  13.6 us (11%)
  local copies, waits for them, and re-layouts  7.02 us (6%)
  between operations  1.71 us (1%)
    dot_general x2, matrix products, expert_rows(): jnp.dot(hidden, weight_out, preferred_element_type=jnp.float32)  47.2 us
    all_to_all x2, starting transfers between devices, on_device(): lax.all_to_all(partials.astype(jnp.bfloat16), 'ex', split_axis=0, concat_...  12 us
    all_to_all x2, starting transfers between devices, on_device(): lax.all_to_all(outgoing, 'ex', split_axis=0, concat_axis=0, tiled=True)  8.68 us
    all_to_all x2, waiting for transfers between devices, on_device(): lax.all_to_all(partials.astype(jnp.bfloat16), 'ex', split_axis=0, concat_...  6.88 us
    ppermute x6, starting transfers between devices, swapped(): return lax.ppermute(value, axis, pairs)  6.55 us
    ppermute x6, waiting for transfers between devices, swapped(): return lax.ppermute(value, axis, pairs)  3.84 us
    unnamed x12, local copies, waits for them, and re-layouts  3.83 us
    broadcast_in_dim x2, other arithmetic, on_device(): jnp.broadcast_to(routed, (EXPERTS, split, row_dev, model))  3.51 us
  transfers between devices with their start and end apart: 10, of which 5 were waited for; matrix products, arithmetic and copies ran while one was open for 54% of the time, Pallas kernels for 0%

commit v1 on v0

v1 whole, which is shorter than its diff:
```python
import functools
import math

import jax
import jax.numpy as jnp
from jax import lax
from jax.experimental import pallas as pl
from jax.experimental.pallas import tpu as pltpu
from jax.sharding import PartitionSpec as P

HD = 128
EXPERTS = 8
BLOCKS = 8
OUT_SLOTS = 5
F32 = jnp.float32
BF16 = jnp.bfloat16


def layer_kernel(
    width,
    q_ref,
    len_ref,
    routes_ref,
    res_ref,
    gain_ref,
    k_hbm,
    v_hbm,
    wr_hbm,
    win_hbm,
    wout_hbm,
    out_ref,
    kbuf,
    vbuf,
    wrbuf,
    winbuf,
    woutbuf,
    lenbuf,
    ctx_out,
    ctx_in,
    gath,
    xbuf,
    hacc,
    hid,
    ykeep,
    pout,
    pin,
    rbuf,
    rin,
    kv_sem,
    win_sem,
    wout_sem,
    len_send,
    len_recv,
    ctx_send,
    ctx_recv,
    ag_send,
    ag_recv,
    fw_send,
    fw_recv,
    pair_send,
    pair_recv,
    ret_send,
    ret_recv,
):
    me = lax.axis_index("ex")
    chips = width // 2
    chip = me // 2
    core = me % 2
    quarter = me % 4
    base = me - quarter
    sibling = me + 1 - 2 * core
    blk = gain_ref.shape[1]
    half = width
    slots = woutbuf.shape[0]

    def same_core(offset):
        return lax.rem(chip + offset, chips) * 2 + core

    def remote(src, dst, send, recv, target):
        return pltpu.make_async_remote_copy(
            src_ref=src,
            dst_ref=dst,
            send_sem=send,
            recv_sem=recv,
            device_id={"ex": target},
            device_id_type=pl.DeviceIdType.MESH,
        )

    barrier = pltpu.get_barrier_semaphore()
    diagonal = base + 3 - quarter

    def greet(device):
        pl.semaphore_signal(
            barrier, inc=1, device_id={"ex": device}, device_id_type=pl.DeviceIdType.MESH
        )

    @pl.loop(1, chips)
    def _(offset):
        greet(same_core(offset))

    greet(sibling)
    greet(diagonal)

    kcopy = pltpu.make_async_copy(k_hbm, kbuf, kv_sem.at[0])
    vcopy = pltpu.make_async_copy(v_hbm, vbuf, kv_sem.at[1])
    wrcopy = pltpu.make_async_copy(wr_hbm, wrbuf, kv_sem.at[2])
    kcopy.start()
    vcopy.start()

    def win_copy(i):
        rows = pl.ds(pl.multiple_of(i * blk, blk), blk)
        return pltpu.make_async_copy(win_hbm.at[0, rows, :], winbuf.at[i], win_sem.at[i])

    def wout_copy(i):
        cols = pl.ds(pl.multiple_of(i * blk, blk), blk)
        return pltpu.make_async_copy(
            wout_hbm.at[0, :, cols], woutbuf.at[lax.rem(i, slots)], wout_sem.at[i]
        )

    @pl.loop(0, BLOCKS)
    def _(i):
        win_copy(i).start()

    wrcopy.start()

    @pl.loop(0, slots)
    def _(i):
        wout_copy(i).start()

    lenbuf[quarter] = jnp.broadcast_to(len_ref[...], lenbuf.shape[1:])
    pl.semaphore_wait(barrier, chips + 1)

    def len_copy(offset):
        peer = lax.rem(quarter + offset, 4)
        return remote(
            lenbuf.at[quarter],
            lenbuf.at[quarter],
            len_send.at[offset],
            len_recv.at[offset],
            base + peer,
        )

    for offset in range(1, 4):
        len_copy(offset).start()

    groups, span = kbuf.shape[1], kbuf.shape[3]
    wide = groups * span
    micros, kv_heads = kbuf.shape[0], kbuf.shape[2]
    per_kv = q_ref.shape[3] // (kv_heads * HD)
    kcopy.wait()
    scores = []
    for m in range(micros):
        query = q_ref[m, 0].astype(F32)
        for h in range(kv_heads):
            rows = jnp.concatenate(
                [
                    query[:, (h * per_kv + j) * HD : (h * per_kv + j + 1) * HD]
                    for j in range(per_kv)
                ],
                axis=0,
            ).astype(BF16)
            keys = kbuf[m, :, h].reshape(wide, HD)
            scores.append(
                lax.dot_general(rows, keys, (((1,), (1,)), ((), ())), preferred_element_type=F32)
                * (1.0 / math.sqrt(HD))
            )
    for offset in range(1, 4):
        len_copy(offset).wait()
    vcopy.wait()
    row_of = lax.broadcasted_iota(jnp.int32, (per_kv * groups, wide), 0) & (groups - 1)
    column = lax.broadcasted_iota(jnp.int32, (per_kv * groups, wide), 1)
    own = row_of == lax.shift_right_logical(column, int(math.log2(span)))
    position = column & (span - 1)
    for m in range(micros):
        used = jnp.concatenate([lenbuf[i, m : m + 1, :] for i in range(groups)], axis=1)
        valid = jnp.logical_and(own, position < used)
        for h in range(kv_heads):
            masked = jnp.where(valid, scores[m * kv_heads + h], -1e30)
            top = jnp.max(masked, axis=-1, keepdims=True)
            expo = jnp.where(valid, jnp.exp(masked - top), 0.0)
            probs = (expo / jnp.sum(expo, axis=-1, keepdims=True)).astype(BF16)
            vals = vbuf[m, :, h].reshape(wide, HD)
            ctx = jnp.dot(probs, vals, preferred_element_type=F32).astype(BF16).astype(F32)
            flat = jnp.concatenate(
                [ctx[j * groups : (j + 1) * groups] for j in range(per_kv)], axis=1
            )
            for i in range(groups):
                ctx_out[i, m * kv_heads + h : m * kv_heads + h + 1, :] = flat[i : i + 1]

    def ctx_copy(offset):
        peer = lax.rem(quarter + offset, 4)
        return remote(
            ctx_out.at[peer],
            ctx_in.at[quarter],
            ctx_send.at[offset],
            ctx_recv.at[offset],
            base + peer,
        )

    for offset in range(1, 4):
        ctx_copy(offset).start()
    ctx_in[quarter] = ctx_out[quarter]
    residual = jnp.concatenate(
        [
            res_ref[m].astype(F32)[:, b * blk : (b + 1) * blk]
            for m in range(micros)
            for b in range(BLOCKS)
        ],
        axis=0,
    )
    for offset in range(1, 4):
        ctx_copy(offset).wait()
    context = jnp.concatenate(
        [
            ctx_in[s, m * kv_heads : (m + 1) * kv_heads, :]
            for m in range(micros)
            for s in range(groups)
        ],
        axis=0,
    )
    state = residual + context
    gain = gain_ref[...]
    pieces = []
    for m in range(micros):
        part = state[m * BLOCKS : (m + 1) * BLOCKS]
        total = jnp.sum(jnp.sum(part * part, axis=1, keepdims=True), axis=0, keepdims=True)
        pieces.append(part * lax.rsqrt(total / (BLOCKS * blk) + 1e-05) * gain)
    normed = jnp.concatenate(pieces, axis=0).astype(BF16)
    gath[me] = normed

    def ag_copy(offset):
        return remote(
            gath.at[me], gath.at[me], ag_send.at[offset], ag_recv.at[offset], same_core(offset)
        )

    def fw_copy(offset):
        source = same_core(chips - offset)
        return remote(
            gath.at[source], gath.at[source], fw_send.at[offset], fw_recv.at[offset], sibling
        )

    @pl.loop(1, chips)
    def _(offset):
        ag_copy(offset).start()

    fw_copy(0).start()

    wrcopy.wait()
    logits = jnp.zeros((micros, EXPERTS), F32)
    for b in range(BLOCKS):
        part = jnp.dot(
            normed, wrbuf[b * blk : (b + 1) * blk, :], preferred_element_type=F32
        )
        logits = logits + jnp.concatenate(
            [part[m * BLOCKS + b : m * BLOCKS + b + 1] for m in range(micros)], axis=0
        )
    gates = jax.nn.sigmoid(logits)
    expert = lax.broadcasted_iota(jnp.int32, (micros, EXPERTS), 1)
    routes = jnp.concatenate([routes_ref[m] for m in range(micros)], axis=0)
    chosen = jnp.zeros((micros, EXPERTS), F32)
    for t in range(routes.shape[1]):
        chosen = chosen + jnp.where(routes[:, t : t + 1] == expert, 1.0, 0.0)
    gates = gates * chosen
    mix = gates / jnp.sum(gates, axis=1, keepdims=True)

    @pl.loop(1, chips)
    def _(offset):
        ag_copy(offset).wait_recv()
        fw_copy(offset).start()

    r = lax.broadcasted_iota(jnp.int32, (256, 256), 0)
    source_row = (((r & 15) >> 1) * 2 + ((r >> 4) & 1)) * 16 + (r & 1) * 8 + (r >> 5)
    order = jnp.where(
        lax.broadcasted_iota(jnp.int32, (256, 256), 1) == source_row, 1.0, 0.0
    ).astype(BF16)

    @pl.loop(0, chips)
    def _(offset):
        fw_copy(offset).wait_recv()

    for g in range(width // 16):
        block = gath[g * 16 : (g + 1) * 16].reshape(256, blk)
        sorted_rows = jnp.dot(order, block, preferred_element_type=F32).astype(BF16)
        for b in range(BLOCKS):
            for c in range(2):
                xbuf[b, c * half + g * 16 : c * half + (g + 1) * 16, :] = sorted_rows[
                    b * 32 + c * 16 : b * 32 + (c + 1) * 16
                ]

    hacc[...] = jnp.zeros_like(hacc)

    @pl.loop(0, BLOCKS)
    def _(i):
        win_copy(i).wait()
        hacc[...] += jnp.dot(xbuf[i], winbuf[i], preferred_element_type=F32)

    pre = hacc[...]
    hid[...] = (pre / (1.0 + jnp.exp(-pre))).astype(BF16)

    def pair_copy(i):
        return remote(pout.at[i], pin.at[i], pair_send.at[i], pair_recv.at[i], sibling)

    def ret_copy(offset, i):
        target = lax.rem(chip + offset, chips)
        return remote(
            rbuf.at[target, i],
            rin.at[chip, i],
            ret_send.at[offset],
            ret_recv.at[offset],
            target * 2 + core,
        )

    def give_back(i):
        pair_copy(i).wait_recv()
        summed = ykeep[lax.rem(i, 2)] + pin[i].astype(F32)
        for t in range(chips):
            rbuf[t, i] = summed[2 * t : 2 * t + 2].astype(BF16)

        @pl.loop(1, chips)
        def _(offset):
            ret_copy(offset, i).start()

        rin[chip, i] = rbuf[chip, i]

    @pl.loop(0, BLOCKS)
    def _(i):
        wout_copy(i).wait()
        part = jnp.dot(hid[...], woutbuf[lax.rem(i, slots)], preferred_element_type=F32)

        @pl.when(i + slots < BLOCKS)
        def _():
            wout_copy(i + slots).start()

        first, second = part[:half], part[half:]
        ykeep[lax.rem(i, 2)] = jnp.where(core == 0, first, second)
        pout[i] = jnp.where(core == 0, second, first).astype(BF16)
        pair_copy(i).start()

        @pl.when(i >= 1)
        def _():
            give_back(i - 1)

    give_back(BLOCKS - 1)

    @pl.loop(1, chips)
    def _(offset):
        ag_copy(offset).wait_send()

    @pl.loop(0, chips)
    def _(offset):
        fw_copy(offset).wait_send()

    @pl.loop(0, BLOCKS)
    def _(i):
        pair_copy(i).wait_send()

    @pl.loop(1, chips)
    def _(offset):
        target = lax.rem(chip + offset, chips)
        source = lax.rem(chip + chips - offset, chips)
        whole = remote(
            rbuf.at[target], rin.at[source], ret_send.at[offset], ret_recv.at[offset], sibling
        )
        whole.wait_send()
        whole.wait_recv()

    split = chips // EXPERTS
    for b in range(BLOCKS):
        total = jnp.concatenate(
            [state[m * BLOCKS + b : m * BLOCKS + b + 1] for m in range(micros)], axis=0
        )
        for x in range(EXPERTS):
            out_x = rin[x * split, b].astype(F32)
            for s in range(1, split):
                out_x = out_x + rin[x * split + s, b].astype(F32)
            total = total + mix[:, x : x + 1] * out_x
        total = total.astype(BF16)
        for m in range(micros):
            out_ref[m, :, b * blk : (b + 1) * blk] = total[m : m + 1]


def on_device(queries, keys, values, lengths, routes, residual, gain, w_router, w_in, w_out):
    width = lax.axis_size("ex")
    chips = width // 2
    micros = queries.shape[0]
    rows = micros * width
    hidden = w_in.shape[2]
    model = residual.shape[2]
    blk = model // BLOCKS
    dma = pltpu.SemaphoreType.DMA
    vmem = pltpu.VMEM
    in_vmem = pl.BlockSpec(memory_space=pltpu.VMEM)
    anywhere = pl.BlockSpec(memory_space=pl.ANY)
    return pl.pallas_call(
        functools.partial(layer_kernel, width),
        out_shape=jax.ShapeDtypeStruct(residual.shape, BF16),
        in_specs=[in_vmem] * 5 + [anywhere] * 5,
        out_specs=in_vmem,
        scratch_shapes=[
            vmem((micros,) + keys.shape[2:], BF16),
            vmem((micros,) + values.shape[2:], BF16),
            vmem(w_router.shape, BF16),
            vmem((BLOCKS, blk, hidden), BF16),
            vmem((OUT_SLOTS, hidden, blk), BF16),
            vmem((4, micros, keys.shape[4]), jnp.int32),
            vmem((4, 4, blk), F32),
            vmem((4, 4, blk), F32),
            vmem((width, 16, blk), BF16),
            vmem((BLOCKS, rows, blk), BF16),
            vmem((rows, hidden), F32),
            vmem((rows, hidden), BF16),
            vmem((2, rows // 2, blk), F32),
            vmem((BLOCKS, rows // 2, blk), BF16),
            vmem((BLOCKS, rows // 2, blk), BF16),
            vmem((chips, BLOCKS, 2, blk), BF16),
            vmem((chips, BLOCKS, 2, blk), BF16),
            dma((3,)),
            dma((BLOCKS,)),
            dma((BLOCKS,)),
            dma((4,)),
            dma((4,)),
            dma((4,)),
            dma((4,)),
            dma((chips,)),
            dma((chips,)),
            dma((chips,)),
            dma((chips,)),
            dma((BLOCKS,)),
            dma((BLOCKS,)),
            dma((chips,)),
            dma((chips,)),
        ],
        compiler_params=pltpu.CompilerParams(
            collective_id=0, has_side_effects=True, vmem_limit_bytes=61 * 1024 * 1024
        ),
    )(
        queries,
        lengths,
        routes,
        residual,
        gain.reshape(BLOCKS, blk).astype(F32),
        keys.reshape((micros,) + keys.shape[2:]),
        values.reshape((micros,) + values.shape[2:]),
        w_router,
        w_in,
        w_out,
    )


def solution(mesh):
    return jax.shard_map(
        on_device,
        mesh=mesh,
        in_specs=(
            P(None, ("grp", "ex"), None, None),
            P(None, ("grp", "ex"), None, None, None, None),
            P(None, ("grp", "ex"), None, None, None, None),
            P(None, ("grp", "ex")),
            P(None, ("grp", "ex"), None),
            P(None, ("grp", "ex"), None),
            P(),
            P(),
            P("ex", None, None),
            P("ex", None, None),
        ),
        out_specs=P(None, ("grp", "ex"), None),
        check_vma=False,
    )
```

time: 119 us -> 49.2 us (0.41)
  matrix products: 52.6 us -> 0 us
  Pallas kernels: 0 us -> 41 us
  starting transfers between devices: 27.2 us -> 0 us
  other arithmetic: 16.3 us -> 0 us
  waiting for transfers between devices: 13.6 us -> 0 us
  between operations: 1.71 us -> 0.01 us
    dot_general x8 -> x0, matrix products: 52.6 us -> none  [the longest x2 47.2 us: expert_rows(): jnp.dot(hidden, weight_out, preferred_element_type=jnp.float32)]
    pallas_call x0 -> x1, Pallas kernels: none -> 41 us  [on_device(): pl.pallas_call(functools.partial(layer_kernel, width), out_shape=jax.Shap...]
    all_to_all x4 -> x0, starting transfers between devices: 20.7 us -> none  [the longest x2 12 us: on_device(): lax.all_to_all(partials.astype(jnp.bfloat16), 'ex', split_axis=0, concat_...]
    all_to_all x4 -> x0, waiting for transfers between devices: 9.76 us -> none  [the longest x2 6.88 us: on_device(): lax.all_to_all(partials.astype(jnp.bfloat16), 'ex', split_axis=0, concat_...]
    ppermute x6 -> x0, starting transfers between devices: 6.55 us -> none  [swapped(): return lax.ppermute(value, axis, pairs)]
    reduce_sum x11 -> x0, other arithmetic: 4.76 us -> none  [the longest x1 1.69 us: on_device(): scale = lax.rsqrt(jnp.mean(state * state, axis=-1, keepdims=True) + 1e-05)]
    broadcast_in_dim x3 -> x0, other arithmetic: 4.22 us -> none  [the longest x2 3.51 us: on_device(): jnp.broadcast_to(routed, (EXPERTS, split, row_dev, model))]
    ppermute x6 -> x0, waiting for transfers between devices: 3.84 us -> none  [swapped(): return lax.ppermute(value, axis, pairs)]
  transfers between devices with their start and end apart: 10 -> 0, of which waited for: 5 -> 0; matrix products, arithmetic and copies ran while one was open for 54% -> 0% of each run, Pallas kernels for 0% -> 0%
where the time goes in v1:
time: 49.2 us; the launch traced here: 48.8 us
  Pallas kernels  41 us (83%)
  local copies, waits for them, and re-layouts  7.74 us (16%)
    pallas_call x1, Pallas kernels, on_device(): pl.pallas_call(functools.partial(layer_kernel, width), out_shape=jax.Shap...  41 us
    unnamed x3, local copies, waits for them, and re-layouts  4.96 us
    pallas_call x1, local copies, waits for them, and re-layouts, on_device(): pl.pallas_call(functools.partial(layer_kernel, width), out_shape=jax.Shap...  1.43 us
    convert_element_type x1, local copies, waits for them, and re-layouts, on_device(): gain.reshape(BLOCKS, blk).astype(F32)  1.35 us

profile of v1, /device:TPU:0, one launch (start us, length us, event | category | flops | bytes accessed | tf_op | source)
XLA Modules:
  0.0 48.8 jit_solution(4282689109218775140)
XLA Ops:
  0.0 1.3 %copy.11.len_ref = s32[2,1]{1,0:T(2,128)} copy(s32[2,1]{0,1:T(1,128)} %param.13) | data formatting | bytes 16 | tf_op args[3]
  1.3 1.3 %reshape.11.gain_ref = f32[8,768]{1,0:T(8,128)} reshape(bf16[6144]{0:T(1024)(128)(2,1)} %param.16) | data formatting | bytes 36864 | tf_op jit(solution)/shard_map/convert_element_type | solution.py:441
  2.6 1.4 %copy.12.res_ref = bf16[2,1,6144]{2,1,0:T(2,128)(2,1)} copy(bf16[2,1,6144]{2,0,1:T(2,128)(2,1)} %param.15) | data formatting | bytes 49152 | tf_op args[5]
  4.0 2.3 %copy.13.wr_hbm = bf16[6144,8]{1,0:T(8,128)(2,1)} copy(bf16[6144,8]{0,1:T(8,128)(2,1)} %param.17) | data formatting | bytes 196608 | tf_op args[7]
  6.3 41.0 %shard_map.100 = bf16[2,1,6144]{2,1,0:T(2,128)(2,1)} custom-call(bf16[2,1,4,1536]{3,2,1,0:T(4,128)(2,1)} %q_ref.1, s32[2,1]{1,0:T(2,128)} %copy.11.len_ref, s32[2,1,4]{2,1,0:T(1,128)} %routes_ref.1, bf16[2,1,6144]{2,1,0:T(2,128)(2,1)} %copy.12.res_ref, f32[8,768]{1,0:T(8,128)} %reshape.11.gain_ref, bf16[2,4,2,256,128]{4,3,2,1,0:T(8,128)(2,1)} %bitcast.2, ...), custom_call_target="tpu_custom_call" | custom-call | tf_op jit(solution)/shard_map/pallas_call | solution.py:394
  47.4 1.4 %copy.14 = bf16[2,1,6144]{2,0,1:T(2,128)(2,1)} copy(bf16[2,1,6144]{2,1,0:T(2,128)(2,1)} %shard_map.100) | data formatting | bytes 49152 | tf_op jit(solution)/shard_map/pallas_call | solution.py:394

commit v2 on v1

--- a/solution.py
+++ b/solution.py
@@ -10,8 +10,10 @@
 
 HD = 128
 EXPERTS = 8
-BLOCKS = 8
-OUT_SLOTS = 5
+BLOCKS = 6
+GROUPS = 3
+PIECES = 8
+OUT_SLOTS = 4
 F32 = jnp.float32
 BF16 = jnp.bfloat16
 
@@ -69,7 +71,10 @@
     quarter = me % 4
     base = me - quarter
     sibling = me + 1 - 2 * core
-    blk = gain_ref.shape[1]
+    blk = gain_ref.shape[0] * gain_ref.shape[1] // BLOCKS
+    piece = blk * BLOCKS // (GROUPS * PIECES)
+    per_blk = blk // piece
+    blk_group = BLOCKS // GROUPS
     half = width
     slots = woutbuf.shape[0]
 
@@ -127,7 +132,10 @@
     def _(i):
         wout_copy(i).start()
 
-    lenbuf[quarter] = jnp.broadcast_to(len_ref[...], lenbuf.shape[1:])
+    for m in range(lenbuf.shape[1]):
+        lenbuf[quarter, m : m + 1, :] = jnp.broadcast_to(
+            len_ref[:, m : m + 1], (1, lenbuf.shape[2])
+        )
     pl.semaphore_wait(barrier, chips + 1)
 
     def len_copy(offset):
@@ -200,59 +208,90 @@
     for offset in range(1, 4):
         ctx_copy(offset).start()
     ctx_in[quarter] = ctx_out[quarter]
-    residual = jnp.concatenate(
+    residual = res_ref[...].astype(F32)
+    gain_rows = gain_ref[...].astype(F32)
+    lanes = piece // HD
+
+    def by_piece(take, g):
+        return jnp.concatenate(
+            [take(m, g * PIECES + k) for m in range(micros) for k in range(PIECES)], axis=0
+        )
+
+    res_parts = [
+        by_piece(lambda m, p: residual[m : m + 1, p * piece : (p + 1) * piece], g)
+        for g in range(GROUPS)
+    ]
+    gains = [
+        by_piece(
+            lambda m, p: jnp.concatenate(
+                [gain_rows[p * lanes + t : p * lanes + t + 1] for t in range(lanes)], axis=1
+            ),
+            g,
+        )
+        for g in range(GROUPS)
+    ]
+    for offset in range(1, 4):
+        ctx_copy(offset).wait()
+    context = ctx_in[...]
+    head_pieces = ctx_in.shape[2] // piece
+
+    def ctx_piece(m, p):
+        head, t = p // head_pieces, p % head_pieces
+        row = m * kv_heads + head % kv_heads
+        return context[head // kv_heads, row : row + 1, t * piece : (t + 1) * piece]
+
+    state = [res_parts[g] + by_piece(ctx_piece, g) for g in range(GROUPS)]
+    squares = sum(jnp.sum(part * part, axis=1, keepdims=True) for part in state)
+    scale = jnp.concatenate(
         [
-            res_ref[m].astype(F32)[:, b * blk : (b + 1) * blk]
+            jnp.broadcast_to(
+                lax.rsqrt(
+                    jnp.sum(squares[m * PIECES : (m + 1) * PIECES], axis=0, keepdims=True)
+                    / (BLOCKS * blk)
+                    + 1e-05
+                ),
+                (PIECES, 1),
+            )
             for m in range(micros)
-            for b in range(BLOCKS)
         ],
         axis=0,
     )
-    for offset in range(1, 4):
-        ctx_copy(offset).wait()
-    context = jnp.concatenate(
-        [
-            ctx_in[s, m * kv_heads : (m + 1) * kv_heads, :]
-            for m in range(micros)
-            for s in range(groups)
-        ],
-        axis=0,
-    )
-    state = residual + context
-    gain = gain_ref[...]
-    pieces = []
-    for m in range(micros):
-        part = state[m * BLOCKS : (m + 1) * BLOCKS]
-        total = jnp.sum(jnp.sum(part * part, axis=1, keepdims=True), axis=0, keepdims=True)
-        pieces.append(part * lax.rsqrt(total / (BLOCKS * blk) + 1e-05) * gain)
-    normed = jnp.concatenate(pieces, axis=0).astype(BF16)
-    gath[me] = normed
-
-    def ag_copy(offset):
+    normed = [(state[g] * scale * gains[g]).astype(BF16) for g in range(GROUPS)]
+    for g in range(GROUPS):
+        gath[me, g] = normed[g]
+
+    parts = (pl.ds(0, 1), pl.ds(1, GROUPS - 1))
+
+    def ag_copy(offset, p):
+        own_part = gath.at[me, parts[p]]
         return remote(
-            gath.at[me], gath.at[me], ag_send.at[offset], ag_recv.at[offset], same_core(offset)
-        )
-
-    def fw_copy(offset):
-        source = same_core(chips - offset)
-        return remote(
-            gath.at[source], gath.at[source], fw_send.at[offset], fw_recv.at[offset], sibling
-        )
-
-    @pl.loop(1, chips)
-    def _(offset):
-        ag_copy(offset).start()
-
-    fw_copy(0).start()
+            own_part, own_part, ag_send.at[p, offset], ag_recv.at[p, offset], same_core(offset)
+        )
+
+    def fw_copy(offset, p):
+        part = gath.at[same_core(chips - offset), parts[p]]
+        return remote(part, part, fw_send.at[p, offset], fw_recv.at[p, offset], sibling)
+
+    for p in range(2):
+
+        @pl.loop(1, chips)
+        def _(offset):
+            ag_copy(offset, p).start()
+
+        fw_copy(0, p).start()
 
     wrcopy.wait()
     logits = jnp.zeros((micros, EXPERTS), F32)
-    for b in range(BLOCKS):
-        part = jnp.dot(
-            normed, wrbuf[b * blk : (b + 1) * blk, :], preferred_element_type=F32
-        )
+    for p in range(GROUPS * PIECES):
+        part = lax.dot_general(
+            normed[p // PIECES],
+            wrbuf[:, p * piece : (p + 1) * piece],
+            (((1,), (1,)), ((), ())),
+            preferred_element_type=F32,
+        )
+        k = p % PIECES
         logits = logits + jnp.concatenate(
-            [part[m * BLOCKS + b : m * BLOCKS + b + 1] for m in range(micros)], axis=0
+            [part[m * PIECES + k : m * PIECES + k + 1] for m in range(micros)], axis=0
         )
     gates = jax.nn.sigmoid(logits)
     expert = lax.broadcasted_iota(jnp.int32, (micros, EXPERTS), 1)
@@ -263,36 +302,61 @@
     gates = gates * chosen
     mix = gates / jnp.sum(gates, axis=1, keepdims=True)
 
-    @pl.loop(1, chips)
-    def _(offset):
-        ag_copy(offset).wait_recv()
-        fw_copy(offset).start()
+    mix_rows = jnp.concatenate(
+        [jnp.broadcast_to(mix[m : m + 1], (PIECES, EXPERTS)) for m in range(micros)], axis=0
+    )
 
     r = lax.broadcasted_iota(jnp.int32, (256, 256), 0)
     source_row = (((r & 15) >> 1) * 2 + ((r >> 4) & 1)) * 16 + (r & 1) * 8 + (r >> 5)
     order = jnp.where(
         lax.broadcasted_iota(jnp.int32, (256, 256), 1) == source_row, 1.0, 0.0
     ).astype(BF16)
-
-    @pl.loop(0, chips)
-    def _(offset):
-        fw_copy(offset).wait_recv()
-
-    for g in range(width // 16):
-        block = gath[g * 16 : (g + 1) * 16].reshape(256, blk)
-        sorted_rows = jnp.dot(order, block, preferred_element_type=F32).astype(BF16)
-        for b in range(BLOCKS):
-            for c in range(2):
-                xbuf[b, c * half + g * 16 : c * half + (g + 1) * 16, :] = sorted_rows[
-                    b * 32 + c * 16 : b * 32 + (c + 1) * 16
-                ]
+    r = lax.broadcasted_iota(jnp.int32, (128, 128), 0)
+    source_row = (r & 7) * 16 + (r >> 4) * 2 + ((r >> 3) & 1)
+    order_back = jnp.where(
+        lax.broadcasted_iota(jnp.int32, (128, 128), 1) == source_row, 1.0, 0.0
+    ).astype(BF16)
+
+    def forward(p):
+        @pl.loop(1, chips)
+        def _(offset):
+            ag_copy(offset, p).wait_recv()
+            fw_copy(offset, p).start()
+
+    def arrived(p):
+        @pl.loop(0, chips)
+        def _(offset):
+            fw_copy(offset, p).wait_recv()
+
+    def sort_rows(g):
+        for w in range(width // 16):
+            block = gath[w * 16 : (w + 1) * 16, g].reshape(256, piece)
+            rows = jnp.dot(order, block, preferred_element_type=F32).astype(BF16)
+            for k in range(PIECES):
+                for c in range(2):
+                    xbuf[g * PIECES + k, c * half + w * 16 : c * half + (w + 1) * 16, :] = rows[
+                        k * 32 + c * 16 : k * 32 + (c + 1) * 16
+                    ]
+
+    def project(i):
+        win_copy(i).wait()
+        rows = jnp.concatenate([xbuf[i * per_blk + t] for t in range(per_blk)], axis=1)
+        hacc[...] += jnp.dot(rows, winbuf[i], preferred_element_type=F32)
 
     hacc[...] = jnp.zeros_like(hacc)
-
-    @pl.loop(0, BLOCKS)
+    forward(0)
+    arrived(0)
+    sort_rows(0)
+    project(0)
+    forward(1)
+    project(1)
+    arrived(1)
+    for g in range(1, GROUPS):
+        sort_rows(g)
+
+    @pl.loop(blk_group, BLOCKS)
     def _(i):
-        win_copy(i).wait()
-        hacc[...] += jnp.dot(xbuf[i], winbuf[i], preferred_element_type=F32)
+        project(i)
 
     pre = hacc[...]
     hid[...] = (pre / (1.0 + jnp.exp(-pre))).astype(BF16)
@@ -300,83 +364,94 @@
     def pair_copy(i):
         return remote(pout.at[i], pin.at[i], pair_send.at[i], pair_recv.at[i], sibling)
 
-    def ret_copy(offset, i):
+    def ret_copy(offset, g):
         target = lax.rem(chip + offset, chips)
         return remote(
-            rbuf.at[target, i],
-            rin.at[chip, i],
-            ret_send.at[offset],
-            ret_recv.at[offset],
+            rbuf.at[g, target],
+            rin.at[g, chip],
+            ret_send.at[g, offset],
+            ret_recv.at[g, offset],
             target * 2 + core,
         )
 
-    def give_back(i):
-        pair_copy(i).wait_recv()
-        summed = ykeep[lax.rem(i, 2)] + pin[i].astype(F32)
-        for t in range(chips):
-            rbuf[t, i] = summed[2 * t : 2 * t + 2].astype(BF16)
+    def expand(i):
+        wout_copy(i).wait()
+        part = jnp.dot(hid[...], woutbuf[lax.rem(i, slots)], preferred_element_type=F32)
+        first, second = part[:half], part[half:]
+        ykeep[i] = jnp.where(core == 0, first, second)
+        pout[i] = jnp.where(core == 0, second, first).astype(BF16)
+        pair_copy(i).start()
+
+    def give_back(g):
+        blocks = range(g * blk_group, (g + 1) * blk_group)
+        for i in blocks:
+            pair_copy(i).wait_recv()
+        summed = [(ykeep[i] + pin[i].astype(F32)).astype(BF16) for i in blocks]
+        for w in range(chips // 8):
+            stacked = jnp.concatenate(
+                [
+                    summed[k // per_blk][
+                        w * 16 : (w + 1) * 16,
+                        (k % per_blk) * piece : (k % per_blk + 1) * piece,
+                    ]
+                    for k in range(PIECES)
+                ],
+                axis=0,
+            )
+            rows = jnp.dot(order_back, stacked, preferred_element_type=F32).astype(BF16)
+            for t in range(8):
+                rbuf[g, w * 8 + t] = rows[t * 16 : (t + 1) * 16]
 
         @pl.loop(1, chips)
         def _(offset):
-            ret_copy(offset, i).start()
-
-        rin[chip, i] = rbuf[chip, i]
-
-    @pl.loop(0, BLOCKS)
-    def _(i):
-        wout_copy(i).wait()
-        part = jnp.dot(hid[...], woutbuf[lax.rem(i, slots)], preferred_element_type=F32)
-
-        @pl.when(i + slots < BLOCKS)
-        def _():
+            ret_copy(offset, g).start()
+
+        rin[g, chip] = rbuf[g, chip]
+
+    for i in range(BLOCKS):
+        expand(i)
+        if i + slots < BLOCKS:
             wout_copy(i + slots).start()
-
-        first, second = part[:half], part[half:]
-        ykeep[lax.rem(i, 2)] = jnp.where(core == 0, first, second)
-        pout[i] = jnp.where(core == 0, second, first).astype(BF16)
-        pair_copy(i).start()
-
-        @pl.when(i >= 1)
-        def _():
-            give_back(i - 1)
-
-    give_back(BLOCKS - 1)
+        if i >= blk_group and i % blk_group == 0:
+            give_back(i // blk_group - 1)
+    give_back(GROUPS - 1)
 
     @pl.loop(1, chips)
     def _(offset):
-        ag_copy(offset).wait_send()
-
-    @pl.loop(0, chips)
-    def _(offset):
-        fw_copy(offset).wait_send()
+        for p in range(2):
+            ag_copy(offset, p).wait_send()
+            fw_copy(offset, p).wait_send()
+
+    for p in range(2):
+        fw_copy(0, p).wait_send()
 
     @pl.loop(0, BLOCKS)
     def _(i):
         pair_copy(i).wait_send()
 
-    @pl.loop(1, chips)
-    def _(offset):
-        target = lax.rem(chip + offset, chips)
-        source = lax.rem(chip + chips - offset, chips)
-        whole = remote(
-            rbuf.at[target], rin.at[source], ret_send.at[offset], ret_recv.at[offset], sibling
-        )
-        whole.wait_send()
-        whole.wait_recv()
-
     split = chips // EXPERTS
-    for b in range(BLOCKS):
-        total = jnp.concatenate(
-            [state[m * BLOCKS + b : m * BLOCKS + b + 1] for m in range(micros)], axis=0
-        )
+    for g in range(GROUPS):
+
+        @pl.loop(1, chips)
+        def _(offset):
+            ret_copy(offset, g).wait()
+
+        total = state[g]
         for x in range(EXPERTS):
-            out_x = rin[x * split, b].astype(F32)
-            for s in range(1, split):
-                out_x = out_x + rin[x * split + s, b].astype(F32)
-            total = total + mix[:, x : x + 1] * out_x
-        total = total.astype(BF16)
-        for m in range(micros):
-            out_ref[m, :, b * blk : (b + 1) * blk] = total[m : m + 1]
+            out_x = rin[g, x * split].astype(F32)
+            for t in range(1, split):
+                out_x = out_x + rin[g, x * split + t].astype(F32)
+            total = total + mix_rows[:, x : x + 1] * out_x
+        flat = jnp.concatenate(
+            [
+                jnp.concatenate(
+                    [total[m * PIECES + k : m * PIECES + k + 1] for m in range(micros)], axis=0
+                )
+                for k in range(PIECES)
+            ],
+            axis=1,
+        )
+        out_ref[:, g * PIECES * piece : (g + 1) * PIECES * piece] = flat.astype(BF16)
 
 
 def on_device(queries, keys, values, lengths, routes, residual, gain, w_router, w_in, w_out):
@@ -387,33 +462,35 @@
     hidden = w_in.shape[2]
     model = residual.shape[2]
     blk = model // BLOCKS
+    piece = model // (GROUPS * PIECES)
+    head = queries.shape[3] // keys.shape[3]
     dma = pltpu.SemaphoreType.DMA
     vmem = pltpu.VMEM
     in_vmem = pl.BlockSpec(memory_space=pltpu.VMEM)
     anywhere = pl.BlockSpec(memory_space=pl.ANY)
     return pl.pallas_call(
         functools.partial(layer_kernel, width),
-        out_shape=jax.ShapeDtypeStruct(residual.shape, BF16),
+        out_shape=jax.ShapeDtypeStruct((micros, model), BF16),
         in_specs=[in_vmem] * 5 + [anywhere] * 5,
         out_specs=in_vmem,
         scratch_shapes=[
             vmem((micros,) + keys.shape[2:], BF16),
             vmem((micros,) + values.shape[2:], BF16),
-            vmem(w_router.shape, BF16),
+            vmem(w_router.shape[::-1], BF16),
             vmem((BLOCKS, blk, hidden), BF16),
             vmem((OUT_SLOTS, hidden, blk), BF16),
             vmem((4, micros, keys.shape[4]), jnp.int32),
-            vmem((4, 4, blk), F32),
-            vmem((4, 4, blk), F32),
-            vmem((width, 16, blk), BF16),
-            vmem((BLOCKS, rows, blk), BF16),
+            vmem((4, 4, head), F32),
+            vmem((4, 4, head), F32),
+            vmem((width, GROUPS, 16, piece), BF16),
+            vmem((GROUPS * PIECES, rows, piece), BF16),
             vmem((rows, hidden), F32),
             vmem((rows, hidden), BF16),
-            vmem((2, rows // 2, blk), F32),
+            vmem((BLOCKS, rows // 2, blk), F32),
             vmem((BLOCKS, rows // 2, blk), BF16),
             vmem((BLOCKS, rows // 2, blk), BF16),
-            vmem((chips, BLOCKS, 2, blk), BF16),
-            vmem((chips, BLOCKS, 2, blk), BF16),
+            vmem((GROUPS, chips, 16, piece), BF16),
+            vmem((GROUPS, chips, 16, piece), BF16),
             dma((3,)),
             dma((BLOCKS,)),
             dma((BLOCKS,)),
@@ -421,30 +498,30 @@
             dma((4,)),
             dma((4,)),
             dma((4,)),
-            dma((chips,)),
-            dma((chips,)),
-            dma((chips,)),
-            dma((chips,)),
+            dma((2, chips)),
+            dma((2, chips)),
+            dma((2, chips)),
+            dma((2, chips)),
             dma((BLOCKS,)),
             dma((BLOCKS,)),
-            dma((chips,)),
-            dma((chips,)),
+            dma((GROUPS, chips)),
+            dma((GROUPS, chips)),
         ],
         compiler_params=pltpu.CompilerParams(
             collective_id=0, has_side_effects=True, vmem_limit_bytes=61 * 1024 * 1024
         ),
     )(
         queries,
-        lengths,
+        lengths.T,
         routes,
-        residual,
-        gain.reshape(BLOCKS, blk).astype(F32),
+        residual.reshape(micros, model),
+        gain.reshape(model // HD, HD),
         keys.reshape((micros,) + keys.shape[2:]),
         values.reshape((micros,) + values.shape[2:]),
-        w_router,
+        w_router.T,
         w_in,
         w_out,
-    )
+    ).reshape(residual.shape)
 
 
 def solution(mesh):

time: 49.2 us -> 41.1 us (0.84)
  local copies, waits for them, and re-layouts: 7.74 us -> 1.36 us
  Pallas kernels: 41 us -> 39.5 us
    unnamed x3 -> x1, local copies, waits for them, and re-layouts: 4.96 us -> 1.36 us
    pallas_call x1, Pallas kernels: 41 us -> 39.5 us  [on_device(): pl.pallas_call(functools.partial(layer_kernel, width), out_shape=jax.Shap...]
    pallas_call x1 -> x0, local copies, waits for them, and re-layouts: 1.43 us -> none  [on_device(): pl.pallas_call(functools.partial(layer_kernel, width), out_shape=jax.Shap...]
    convert_element_type x1 -> x0, local copies, waits for them, and re-layouts: 1.35 us -> none  [on_device(): gain.reshape(BLOCKS, blk).astype(F32)]
where the time goes in v2:
time: 41.1 us; the launch traced here: 40.8 us
  Pallas kernels  39.5 us (96%)
  local copies, waits for them, and re-layouts  1.36 us (3%)
    pallas_call x1, Pallas kernels, on_device(): pl.pallas_call(functools.partial(layer_kernel, width), out_shape=jax.Shap...  39.5 us
    unnamed x1, local copies, waits for them, and re-layouts  1.36 us

profile of v2, /device:TPU:0, one launch (start us, length us, event | category | flops | bytes accessed | tf_op | source)
XLA Modules:
  0.0 40.8 jit_solution(2962607942061504261)
XLA Ops:
  0.0 39.5 %shard_map.100 = bf16[2,6144]{1,0:T(2,128)(2,1)} custom-call(bf16[2,1,4,1536]{3,2,1,0:T(4,128)(2,1)} %q_ref.1, s32[1,2]{1,0:T(1,128)} %bitcast.13, s32[2,1,4]{2,1,0:T(1,128)} %routes_ref.1, bf16[2,6144]{1,0:T(2,128)(2,1)} %bitcast.11, bf16[48,128]{1,0:T(8,128)(2,1)} %bitcast.12, bf16[2,4,2,256,128]{4,3,2,1,0:T(8,128)(2,1)} %bitcast.7, ...), custom_call_target="tpu_custom_call" | custom-call | tf_op jit(solution)/shard_map/pallas_call | solution.py:471
  39.5 1.4 %copy.12 = bf16[2,1,6144]{2,0,1:T(2,128)(2,1)} copy(bf16[2,1,6144]{2,0,1:T(2,128)(2,1)} %bitcast.10) | data formatting | bytes 49152

commit v3 on v2

--- a/solution.py
+++ b/solution.py
@@ -126,12 +126,6 @@
     def _(i):
         win_copy(i).start()
 
-    wrcopy.start()
-
-    @pl.loop(0, slots)
-    def _(i):
-        wout_copy(i).start()
-
     for m in range(lenbuf.shape[1]):
         lenbuf[quarter, m : m + 1, :] = jnp.broadcast_to(
             len_ref[:, m : m + 1], (1, lenbuf.shape[2])
@@ -150,6 +144,12 @@
 
     for offset in range(1, 4):
         len_copy(offset).start()
+
+    wrcopy.start()
+
+    @pl.loop(0, slots)
+    def _(i):
+        wout_copy(i).start()
 
     groups, span = kbuf.shape[1], kbuf.shape[3]
     wide = groups * span
@@ -280,32 +280,6 @@
 
         fw_copy(0, p).start()
 
-    wrcopy.wait()
-    logits = jnp.zeros((micros, EXPERTS), F32)
-    for p in range(GROUPS * PIECES):
-        part = lax.dot_general(
-            normed[p // PIECES],
-            wrbuf[:, p * piece : (p + 1) * piece],
-            (((1,), (1,)), ((), ())),
-            preferred_element_type=F32,
-        )
-        k = p % PIECES
-        logits = logits + jnp.concatenate(
-            [part[m * PIECES + k : m * PIECES + k + 1] for m in range(micros)], axis=0
-        )
-    gates = jax.nn.sigmoid(logits)
-    expert = lax.broadcasted_iota(jnp.int32, (micros, EXPERTS), 1)
-    routes = jnp.concatenate([routes_ref[m] for m in range(micros)], axis=0)
-    chosen = jnp.zeros((micros, EXPERTS), F32)
-    for t in range(routes.shape[1]):
-        chosen = chosen + jnp.where(routes[:, t : t + 1] == expert, 1.0, 0.0)
-    gates = gates * chosen
-    mix = gates / jnp.sum(gates, axis=1, keepdims=True)
-
-    mix_rows = jnp.concatenate(
-        [jnp.broadcast_to(mix[m : m + 1], (PIECES, EXPERTS)) for m in range(micros)], axis=0
-    )
-
     r = lax.broadcasted_iota(jnp.int32, (256, 256), 0)
     source_row = (((r & 15) >> 1) * 2 + ((r >> 4) & 1)) * 16 + (r & 1) * 8 + (r >> 5)
     order = jnp.where(
@@ -415,6 +389,32 @@
         if i >= blk_group and i % blk_group == 0:
             give_back(i // blk_group - 1)
     give_back(GROUPS - 1)
+
+    wrcopy.wait()
+    logits = jnp.zeros((micros, EXPERTS), F32)
+    for p in range(GROUPS * PIECES):
+        part = lax.dot_general(
+            normed[p // PIECES],
+            wrbuf[:, p * piece : (p + 1) * piece],
+            (((1,), (1,)), ((), ())),
+            preferred_element_type=F32,
+        )
+        k = p % PIECES
+        logits = logits + jnp.concatenate(
+            [part[m * PIECES + k : m * PIECES + k + 1] for m in range(micros)], axis=0
+        )
+    gates = jax.nn.sigmoid(logits)
+    expert = lax.broadcasted_iota(jnp.int32, (micros, EXPERTS), 1)
+    routes = jnp.concatenate([routes_ref[m] for m in range(micros)], axis=0)
+    chosen = jnp.zeros((micros, EXPERTS), F32)
+    for t in range(routes.shape[1]):
+        chosen = chosen + jnp.where(routes[:, t : t + 1] == expert, 1.0, 0.0)
+    gates = gates * chosen
+    mix = gates / jnp.sum(gates, axis=1, keepdims=True)
+
+    mix_rows = jnp.concatenate(
+        [jnp.broadcast_to(mix[m : m + 1], (PIECES, EXPERTS)) for m in range(micros)], axis=0
+    )
 
     @pl.loop(1, chips)
     def _(offset):

time: 41.1 us -> 41.2 us (level)
  no operation moved by 1% of the time
where the time goes in v3:
time: 41.2 us; the launch traced here: 41 us
  Pallas kernels  39.6 us (96%)
  local copies, waits for them, and re-layouts  1.36 us (3%)
    pallas_call x1, Pallas kernels, on_device(): pl.pallas_call(functools.partial(layer_kernel, width), out_shape=jax.Shap...  39.6 us
    unnamed x1, local copies, waits for them, and re-layouts  1.36 us

profile of v3, /device:TPU:0, one launch (start us, length us, event | category | flops | bytes accessed | tf_op | source)
XLA Modules:
  0.0 41.0 jit_solution(15234620141422812067)
XLA Ops:
  0.0 39.6 %shard_map.100 = bf16[2,6144]{1,0:T(2,128)(2,1)} custom-call(bf16[2,1,4,1536]{3,2,1,0:T(4,128)(2,1)} %q_ref.1, s32[1,2]{1,0:T(1,128)} %bitcast.13, s32[2,1,4]{2,1,0:T(1,128)} %routes_ref.1, bf16[2,6144]{1,0:T(2,128)(2,1)} %bitcast.11, bf16[48,128]{1,0:T(8,128)(2,1)} %bitcast.12, bf16[2,4,2,256,128]{4,3,2,1,0:T(8,128)(2,1)} %bitcast.7, ...), custom_call_target="tpu_custom_call" | custom-call | tf_op jit(solution)/shard_map/pallas_call | solution.py:471
  39.6 1.4 %copy.12 = bf16[2,1,6144]{2,0,1:T(2,128)(2,1)} copy(bf16[2,1,6144]{2,0,1:T(2,128)(2,1)} %bitcast.10) | data formatting | bytes 49152
